TPU v7x, 256 devices: a whole 4x4x8 slice. The times are simulated.
256 devices in a mesh: date: 8 (over x, y_hi), rng: 32 (over z, y_lo, core).
Axes of the slice: x: 4, y: 4 (y_hi: 2, y_lo: 2; y = y_hi * 2 + y_lo), z: 8, core: 2. Of those that a mesh axis runs over, the one named last changes fastest.
Arguments:
- slc: bfloat16 [2, 32, 256, 16384], P(None, 'date', None, 'rng'), may hold values from -6 to 6
- shift_table: int32 [32, 16384], P('date', 'rng'), may hold values from -189 to 188
- phase_table: int32 [32, 16384], P('date', 'rng'), may hold values from 0 to 255
- reference_ids: int32 [2], replicated, may hold values from 0 to 31
Outputs:
- multilook: float32 [2, 32, 64, 1024], P(None, 'date', None, 'rng')
- coherence: float32 [32, 64, 1024], P('date', None, 'rng')
All inputs are finite; a program needn't handle non-finite values.
Results may differ from a plain program's by a relative error of at most 0.0041.
Values may be sent and summed in bfloat16 or wider, within the bound.
A program may use at most 128 MiB of HBM per device.

v0:
```python
import jax
import jax.numpy as jnp
from jax import lax
from jax.sharding import PartitionSpec as P

HALO = 192
TAPS = 8
PHASES = 256
LOOK_AZ = 4
LOOK_RG = 16
MS_DEVS = 4


def from_root(block, axis, owner):
    block = jnp.where(lax.axis_index(axis) == owner, block, jnp.zeros_like(block))
    return lax.psum(block, axis)


def extended(x, sides, width):
    for axis, dim in sides:
        peers, length = (lax.axis_size(axis), x.shape[dim])
        up = [(i, (i + 1) % peers) for i in range(peers - 1)]
        down = [(j, i) for i, j in up]
        last = lax.slice_in_dim(x, length - width, length, axis=dim)
        leading = lax.slice_in_dim(x, 0, width, axis=dim)
        before = lax.ppermute(last, axis, up)
        after = lax.ppermute(leading, axis, down)
        x = jnp.concatenate([before, x, after], axis=dim)
    return x


def kernel_table():
    fraction = jnp.arange(PHASES, dtype=jnp.float32) / PHASES
    tap_offset = jnp.arange(TAPS, dtype=jnp.float32) - (TAPS // 2 - 1)
    distance = tap_offset[:, None] - fraction[None, :]
    weight = jnp.sinc(distance) * (0.5 + 0.5 * jnp.cos(jnp.pi * distance / (TAPS // 2 + 1)))
    return weight / jnp.sum(weight, axis=0, keepdims=True)


def band_matrix(shifts, phases, kernel):
    width = shifts.shape[0]
    onehot = (phases[None, :] == jnp.arange(PHASES, dtype=jnp.int32)[:, None]).astype(jnp.float32)
    coefficients = jnp.dot(kernel, onehot, precision=lax.Precision.HIGHEST)
    first_tap = jnp.arange(width, dtype=jnp.int32) + shifts + (HALO - TAPS // 2 + 1)
    source = jnp.arange(width + 2 * HALO, dtype=jnp.int32)[:, None]
    offset = source - first_tap[None, :]
    band = jnp.zeros((width + 2 * HALO, width), jnp.float32)
    for k in range(TAPS):
        band = band + jnp.where(offset == k, coefficients[k][None, :], 0.0)
    return band


def resample_window(window, shifts, phases, kernel):
    width = shifts.shape[0]
    band = band_matrix(shifts, phases, kernel)
    flat = window.reshape(-1, window.shape[-1]).astype(jnp.float32)
    summed = jnp.dot(flat, band, precision=lax.Precision.HIGHEST)
    return summed.reshape(window.shape[:-1] + (width,)).astype(jnp.bfloat16)


def resample_stack(padded, shifts, phases, kernel):
    dates_here = shifts.shape[0]
    outputs = [
        resample_window(padded[:, d], shifts[d], phases[d], kernel) for d in range(dates_here)
    ]
    return jnp.stack(outputs, axis=1)


def patch_sum(v):
    n, lines, pixels = v.shape
    return v.reshape(n, lines // LOOK_AZ, LOOK_AZ, pixels // LOOK_RG, LOOK_RG).sum(axis=(2, 4))


def patch_stats(dates, ref_tile):
    date_re = dates[0].astype(jnp.float32)
    date_im = dates[1].astype(jnp.float32)
    ref_re = ref_tile[0].astype(jnp.float32)[None]
    ref_im = ref_tile[1].astype(jnp.float32)[None]
    ifg_re = date_re * ref_re + date_im * ref_im
    ifg_im = date_im * ref_re - date_re * ref_im
    power_a = date_re * date_re + date_im * date_im
    power_b = ref_re * ref_re + ref_im * ref_im
    sum_re = patch_sum(ifg_re)
    sum_im = patch_sum(ifg_im)
    sum_a = patch_sum(power_a)
    sum_b = patch_sum(power_b)
    multilook = jnp.stack([sum_re, sum_im]) / (LOOK_AZ * LOOK_RG)
    coherence = jnp.sqrt(sum_re * sum_re + sum_im * sum_im) / jnp.sqrt(sum_a * sum_b + 1e-06)
    return (multilook, coherence)


def share_references(owned, reference_ids, zero_tile, groups, dates_dev, my_stack):

    def share_step(m, held_ref):
        owner = reference_ids[m] // dates_dev
        received = from_root(owned(m), "date", owner)
        return jnp.where(m == my_stack, received, held_ref)

    return lax.fori_loop(0, groups, share_step, zero_tile)


def on_device(slc, shift_table, phase_table, reference_ids):
    kernel = kernel_table()
    padded = extended(slc, (("rng", 3),), HALO)
    shifts, phases = (shift_table, phase_table)
    dates_dev = slc.shape[1]
    groups = lax.axis_size("date") // MS_DEVS
    my_stack = lax.axis_index("date") // MS_DEVS
    zero_tile = jnp.zeros((2, padded.shape[2], shifts.shape[1]), jnp.bfloat16)
    resampled = resample_stack(padded, shifts, phases, kernel)

    def owned(m):
        slot_index = reference_ids[m] % dates_dev
        return lax.dynamic_index_in_dim(resampled, slot_index, 1, keepdims=False)

    ref_tile = share_references(owned, reference_ids, zero_tile, groups, dates_dev, my_stack)
    multilook, coherence = patch_stats(resampled, ref_tile)
    return (multilook, coherence)


def solution(mesh):
    placed = (P(None, "date", None, "rng"), P("date", "rng"), P("date", "rng"), P())
    return jax.shard_map(
        on_device,
        mesh=mesh,
        in_specs=placed,
        out_specs=(P(None, "date", None, "rng"), P("date", None, "rng")),
        check_vma=False,
    )
```

profile of v0, /device:TPU:8, one launch (start us, length us, event | category | flops | bytes accessed | tf_op | source)
XLA Modules:
  0.0 304.3 jit_solution(4333898554904256543)
XLA Ops:
  7.2 2.0 fusion.348
  9.2 0.5 copy.26
  9.8 1.9 collective-permute-start
  11.7 1.3 copy.27
  12.9 3.6 %collective-permute-start.1 = (bf16[2,4,256,192]{2,3,1,0:T(8,128)(2,1)}, bf16[2,4,256,192]{2,3,1,0:T(8,128)(2,1)}, u32[]{:S(2)}, u32[]{:S(2)}) collective-permute-start(bf16[2,4,256,192]{2,3,1,0:T(8,128)(2,1)} %copy.27), channel_id=1, source_target_pairs={{1,0},{2,1},{3,2},{4,3},{5,4},{6,5},{7,6},{8,7},{9,8},{10,9},{11,1... | collective-permute-start | bytes 2359304 | tf_op jit(solution)/shard_map/ppermute | solution.py:27
  18.3 13.3 %collective-permute-done = bf16[2,4,256,192]{2,3,1,0:T(8,128)(2,1)} collective-permute-done((bf16[2,4,256,192]{2,3,1,0:T(8,128)(2,1)S(1)}, bf16[2,4,256,192]{2,3,1,0:T(8,128)(2,1)}, u32[]{:S(2)}, u32[]{:S(2)}) %collective-permute-start) | collective-permute-done | bytes 786464 | tf_op jit(solution)/shard_map/ppermute | solution.py:26
  31.6 2.2 copy.21
  33.8 2.2 copy.23
  36.0 3.8 %pad_maximum_fusion = bf16[2,4,256,896]{3,2,0,1:T(8,128)(2,1)S(1)} fusion(bf16[2,4,256,192]{3,2,0,1:T(8,128)(2,1)} %copy.23, bf16[2,4,256,192]{3,2,0,1:T(8,128)(2,1)} %copy.21, bf16[2,4,256,512]{3,2,1,0:T(8,128)(2,1)S(1)} %copy-done.1), kind=kLoop, calls=%fused_computation.5 | loop fusion | flops 11010048 | bytes 7340032 | tf_op jit(solution)/shard_map/concatenate | solution.py:28
  39.9 3.5 %fusion.147 = bf16[2,1,256,512]{3,2,0,1:T(8,128)(2,1)S(1)} fusion(bf16[2,4,256,896]{3,2,0,1:T(8,128)(2,1)S(1)} %pad_maximum_fusion, f32[512]{0:T(512)S(1)} %bitcast.108, f32[512]{0:T(512)S(1)} %bitcast.109, f32[512]{0:T(512)S(1)} %bitcast.110, f32[512]{0:T(512)S(1)} %bitcast.111, f32[512]{0:T(512)S(1)} %bitcast.112, f32[512]{0:T(512)S(1)} %bitcast.113, ...), kind=kOutput, calls=%fused_computation.116 | convolution fusion | flops 2829844480 | bytes 1460224 | tf_op jit(solution)/shard_map/dot_general | solution.py:57
  43.3 3.5 %fusion.150 = bf16[2,1,256,512]{3,2,0,1:T(8,128)(2,1)S(1)} fusion(bf16[2,4,256,896]{3,2,0,1:T(8,128)(2,1)S(1)} %pad_maximum_fusion, f32[512]{0:T(512)S(1)} %bitcast.132, f32[512]{0:T(512)S(1)} %bitcast.133, f32[512]{0:T(512)S(1)} %bitcast.134, f32[512]{0:T(512)S(1)} %bitcast.135, f32[512]{0:T(512)S(1)} %bitcast.136, f32[512]{0:T(512)S(1)} %bitcast.137, ...), kind=kOutput, calls=%fused_computation.117 | convolution fusion | flops 2829844480 | bytes 1460224 | tf_op jit(solution)/shard_map/dot_general | solution.py:57
  46.8 3.5 %fusion.153 = bf16[2,1,256,512]{3,2,0,1:T(8,128)(2,1)S(1)} fusion(bf16[2,4,256,896]{3,2,0,1:T(8,128)(2,1)S(1)} %pad_maximum_fusion, f32[512]{0:T(512)S(1)} %bitcast.124, f32[512]{0:T(512)S(1)} %bitcast.125, f32[512]{0:T(512)S(1)} %bitcast.126, f32[512]{0:T(512)S(1)} %bitcast.127, f32[512]{0:T(512)S(1)} %bitcast.128, f32[512]{0:T(512)S(1)} %bitcast.129, ...), kind=kOutput, calls=%fused_computation.118 | convolution fusion | flops 2829844480 | bytes 1460224 | tf_op jit(solution)/shard_map/dot_general | solution.py:57
  50.3 3.7 %fusion.144 = bf16[2,1,256,512]{3,2,0,1:T(8,128)(2,1)S(1)} fusion(bf16[2,4,256,896]{3,2,0,1:T(8,128)(2,1)S(1)} %pad_maximum_fusion, f32[512]{0:T(512)S(1)} %bitcast.116, f32[512]{0:T(512)S(1)} %bitcast.117, f32[512]{0:T(512)S(1)} %bitcast.118, f32[512]{0:T(512)S(1)} %bitcast.119, f32[512]{0:T(512)S(1)} %bitcast.120, f32[512]{0:T(512)S(1)} %bitcast.121, ...), kind=kOutput, calls=%fused_computation.115 | convolution fusion | flops 2829844480 | bytes 1460224 | tf_op jit(solution)/shard_map/dot_general | solution.py:57
  54.3 2.5 slice_convert_fusion.1
  56.8 189.5 %while.16 = (s32[]{:T(128)}, bf16[2,256,512]{2,1,0:T(8,128)(2,1)S(1)}, s32[]{:T(128)}, s32[2]{0:T(128)S(1)}, bf16[2,4,256,512]{3,2,0,1:T(8,128)(2,1)S(1)}, /*ind...) while((s32[]{:T(128)}, ...), condition=%wide.region_3.4_spmd.clone, body=%wide.region_1.3_spmd.clone.sunk | while | flops 1048606 | bytes 5767640 | solution.py:99
  56.8 0.6 dynamic_slice.28
  59.9 0.8 select_bitcast_fusion.2
  60.8 92.5 %all-reduce.2.cloned.1.call-done = bf16[2,256,512]{2,1,0:T(8,128)(2,1)} async-done(((bf16[2,256,512]{2,1,0:T(8,128)(2,1)}), bf16[2,256,512]{2,1,0:T(8,128)(2,1)}) %all-reduce.2.cloned.1.call-update) | async-done | bytes 524304 | tf_op jit(solution)/shard_map/while/body/eval_jaxpr/psum | solution.py:16
  153.3 1.2 select_select_fusion.2
  154.6 0.6 dynamic_slice.28
  157.7 0.8 select_bitcast_fusion.2
  158.6 87.5 %all-reduce.2.cloned.1.call-done = bf16[2,256,512]{2,1,0:T(8,128)(2,1)} async-done(((bf16[2,256,512]{2,1,0:T(8,128)(2,1)}), bf16[2,256,512]{2,1,0:T(8,128)(2,1)}) %all-reduce.2.cloned.1.call-update) | async-done | bytes 524304 | tf_op jit(solution)/shard_map/while/body/eval_jaxpr/psum | solution.py:16
  246.5 0.9 multiply_add_fusion
  247.4 10.8 %reshape.78 = f32[4,64,4,32,16]{4,3,2,1,0:T(8,128)} reshape(f32[1,4,256,512]{3,2,0,1:T(8,128)} %get-tuple-element.173) | data formatting | bytes 4194304 | tf_op jit(solution)/shard_map/convert_element_type | solution.py:75
  258.2 8.9 %reshape.79 = f32[4,64,4,32,16]{4,3,2,1,0:T(8,128)} reshape(f32[1,4,256,512]{3,2,0,1:T(8,128)S(1)} %copy-done) | data formatting | bytes 4194304 | tf_op jit(solution)/shard_map/convert_element_type | solution.py:76
  267.1 2.8 mul.191
  269.8 2.8 mul.194
  272.7 2.7 reshape.77
  275.4 2.6 reduce_sum.49
  277.9 18.0 %add_reduce_fusion.1 = (f32[4,64,32]{2,1,0:T(8,128)S(1)}, f32[4,64,32]{2,1,0:T(8,128)S(1)}, f32[4,64,32]{2,1,0:T(8,128)S(1)}) fusion(f32[4,64,4,32,16]{4,3,2,1,0:T(8,128)} %reshape.79, f32[4,64,4,32,16]{4,3,2,1,0:T(8,128)} %reshape.78, f32[64,4,32,16]{3,2,1,0:T(8,128)} %mul.194, f32[64,4,32,16]{3,2,1,0:T(8,128)} %mul.191), kind=kLoop, calls=%fused_computation.4 | loop fusion | flops 6266880 | bytes 5341184 | tf_op jit(solution)/shard_map/reduce_sum | solution.py:71
  296.0 0.7 copy.25
  296.7 0.8 copy.24
  (36 shorter events, 2.4 us)
Async XLA Ops:
  9.2 7.4 %copy-start.3 = (s32[4,512]{1,0:T(4,128)S(1)}, s32[4,512]{1,0:T(4,128)}, u32[]{:S(2)}) copy-start(s32[4,512]{1,0:T(4,128)} %param.8) | copy-start | bytes 24580
  9.7 8.4 %copy-start.4 = (s32[4,512]{1,0:T(4,128)S(1)}, s32[4,512]{1,0:T(4,128)}, u32[]{:S(2)}) copy-start(s32[4,512]{1,0:T(4,128)} %param.7) | copy-start | bytes 24580
  9.8 21.8 %collective-permute-start = (bf16[2,4,256,192]{2,3,1,0:T(8,128)(2,1)S(1)}, bf16[2,4,256,192]{2,3,1,0:T(8,128)(2,1)}, u32[]{:S(2)}, u32[]{:S(2)}) collective-permute-start(bf16[2,4,256,192]{2,3,1,0:T(8,128)(2,1)S(1)} %copy.26), channel_id=1, source_target_pairs={{0,1},{1,2},{2,3},{3,4},{4,5},{5,6},{6,7},{7,8},{8,9},{9,10},{10,1... | collective-permute-start | bytes 2359304 | tf_op jit(solution)/shard_map/ppermute | solution.py:26
  12.9 20.9 %collective-permute-start.1 = (bf16[2,4,256,192]{2,3,1,0:T(8,128)(2,1)}, bf16[2,4,256,192]{2,3,1,0:T(8,128)(2,1)}, u32[]{:S(2)}, u32[]{:S(2)}) collective-permute-start(bf16[2,4,256,192]{2,3,1,0:T(8,128)(2,1)} %copy.27), channel_id=1, source_target_pairs={{1,0},{2,1},{3,2},{4,3},{5,4},{6,5},{7,6},{8,7},{9,8},{10,9},{11,1... | collective-permute-start | bytes 2359304 | tf_op jit(solution)/shard_map/ppermute | solution.py:27
  18.3 17.8 %copy-start.1 = (bf16[2,4,256,512]{3,2,1,0:T(8,128)(2,1)S(1)}, bf16[2,4,256,512]{3,2,1,0:T(8,128)(2,1)}, u32[]{:S(2)}) copy-start(bf16[2,4,256,512]{3,2,1,0:T(8,128)(2,1)} %param.6) | copy-start | bytes 6291460
  54.3 2.5 copy-start.5
  56.8 96.5 %all-reduce.2.cloned.1.call-start = ((), (), s32[]{:S(2)}) async-start(), calls=%async_computation | async-start | bytes 1048576 | tf_op jit(solution)/shard_map/while/body/eval_jaxpr/psum | solution.py:16
  154.6 91.5 %all-reduce.2.cloned.1.call-start = ((), (), s32[]{:S(2)}) async-start(), calls=%async_computation | async-start | bytes 1048576 | tf_op jit(solution)/shard_map/while/body/eval_jaxpr/psum | solution.py:16
  247.4 10.8 %copy-start = (f32[1,4,256,512]{3,2,0,1:T(8,128)S(1)}, f32[1,4,256,512]{3,2,0,1:T(8,128)}, u32[]{:S(2)}) copy-start(f32[1,4,256,512]{3,2,0,1:T(8,128)} %get-tuple-element.174) | copy-start | bytes 6291460
  269.8 2.8 copy-start.2
Sparse Core Ops, SparseCore 0:
  60.9 92.3 all-reduce.1
  158.7 87.3 all-reduce.1
where the time goes:
time: 306 us; the launch traced here: 304 us
  waiting for transfers between devices  193 us (63%)
  local copies, waits for them, and re-layouts  39.1 us (13%)
  other arithmetic  31.5 us (10%)
  matrix products  15.4 us (5%)
  between operations  14.2 us (5%)
  starting transfers between devices  5.6 us (2%)
  loops' own time  5.08 us (2%)
    psum x2, waiting for transfers between devices, from_root(): return lax.psum(block, axis)  180 us
    reduce_sum x2, other arithmetic, patch_sum(): v.reshape(n, lines // LOOK_AZ, LOOK_AZ, pixels // LOOK_RG, LOOK_RG)  20.5 us
    dot_general x4, matrix products, resample_window(): summed = jnp.dot(flat, band, precision=lax.Precision.HIGHEST)  14.1 us
    ppermute x1, waiting for transfers between devices, extended(): before = lax.ppermute(last, axis, up)  13.3 us
    convert_element_type x1, local copies, waits for them, and re-layouts, patch_stats(): date_re = dates[0].astype(jnp.float32)  10.8 us
    convert_element_type x1, local copies, waits for them, and re-layouts, patch_stats(): date_im = dates[1].astype(jnp.float32)  8.91 us
  transfers between devices with their start and end apart: 4, of which 3 were waited for; matrix products, arithmetic and copies ran while one was open for 2% of the time, Pallas kernels for 0%

commit v1 on v0

v1 whole, which is shorter than its diff:
```python
import functools

import jax
import jax.numpy as jnp
import numpy as np
from jax import lax
from jax.experimental import pallas as pl
from jax.experimental.pallas import tpu as pltpu
from jax.sharding import PartitionSpec as P

TAPS = 8
PHASES = 256
LOOK_AZ = 4
LOOK_RG = 16
CHUNKS = 4
WIN = 768
MESH = pl.DeviceIdType.MESH
BF16 = jnp.bfloat16
F32 = jnp.float32


def tap_table():
    fraction = np.arange(PHASES) / PHASES
    tap_offset = np.arange(TAPS) - (TAPS // 2 - 1)
    t = tap_offset[:, None] - fraction[None, :]
    weight = np.sinc(t) * (0.5 + 0.5 * np.cos(np.pi * t / (TAPS // 2 + 1)))
    weight = jnp.asarray(weight / weight.sum(axis=0, keepdims=True), F32)
    high = weight.astype(BF16)
    low = (weight - high.astype(F32)).astype(BF16)
    return jnp.concatenate([high, low], axis=0)


def half_turn(v):
    return pltpu.roll(v.astype(F32), 64, 1).astype(BF16)


def two_rows(v):
    return v.reshape(-1, v.shape[-1])


def kernel(
    dates, rngs, chunks, half_lines,
    ids, shift_ref, phase_ref, table_ref, slc_hbm,
    ml_ref, coh_ref,
    own, near_send, far_send, near_recv, far_recv, band_hi, band_lo,
    resampled, outer_in, outer_sel, inner_in, inner_sel, cross_in, final_own, final_in,
    lane_sums, looks,
    own_sem, halo_send, halo_recv, ref_send, ref_recv,
):
    rows = half_lines // chunks
    me_d, me_r = lax.axis_index("date"), lax.axis_index("rng")
    x, yh = me_d // 2, me_d % 2
    outer_x = 3 - x
    inner_x = x + 1 - 2 * (x % 2)
    half = x % 2
    left, right = (me_r + rngs - 1) % rngs, (me_r + 1) % rngs
    stack = x // 2
    dev_outer = (outer_x * 2 + yh, me_r)
    dev_inner = (inner_x * 2 + yh, me_r)
    dev_cross = (x * 2 + 1 - yh, me_r)
    dev_left, dev_right = (me_d, left), (me_d, right)

    load = pltpu.make_async_copy(slc_hbm, own, own_sem)
    load.start()
    barrier = pltpu.get_barrier_semaphore()
    for device in (dev_left, dev_right, dev_outer, dev_inner, dev_cross):
        pl.semaphore_signal(barrier, inc=1, device_id=device, device_id_type=MESH)

    mine = jnp.where(stack == 0, ids[0], ids[1])
    other = jnp.where(stack == 0, ids[1], ids[0])
    slot_m, slot_o = mine % 4, other % 4
    p0 = slot_o
    same = slot_m == slot_o
    p1 = jnp.where(same, (slot_o + 1) % 4, slot_m)
    p2 = jnp.where((p0 != 0) & (p1 != 0), 0, jnp.where((p0 != 1) & (p1 != 1), 1, 2))
    p3 = 6 - p0 - p1 - p2
    order = (p0, p1, p2, p3)
    mine_at = jnp.where(same, 0, 1)
    owner = mine // 4
    owner_x, owner_yh = owner // 2, owner % 2

    lane = lax.broadcasted_iota(jnp.int32, (1, 128), 1)

    def stage(i):
        for re_im in range(2):
            near_send[0, i, re_im] = own[re_im, order[i], :, :, 384:512]
            near_send[1, i, re_im] = own[re_im, order[i], :, :, 0:128]
        for h in range(2):
            re = own[0, order[i], h, :, 256:384].astype(F32)
            im = own[1, order[i], h, :, 256:384].astype(F32)
            far_send[0, i, h] = jnp.where(lane < 64, pltpu.roll(re, 64, 1), im).astype(BF16)
            re = own[0, order[i], h, :, 128:256].astype(F32)
            im = own[1, order[i], h, :, 128:256].astype(F32)
            far_send[1, i, h] = jnp.where(lane < 64, re, pltpu.roll(im, 64, 1)).astype(BF16)

    def halo(group, j):
        at = pl.ds(j * rows, rows)
        pair = pl.ds(2 * group, 2)
        copies = []
        for side, device in enumerate((dev_right, dev_left)):
            copies.append(pltpu.make_async_remote_copy(
                src_ref=near_send.at[side, pair, :, :, at, :],
                dst_ref=near_recv.at[side, pair, :, :, at, :],
                send_sem=halo_send.at[group, j, side, 0],
                recv_sem=halo_recv.at[group, j, side, 0],
                device_id=device, device_id_type=MESH))
            copies.append(pltpu.make_async_remote_copy(
                src_ref=far_send.at[side, pair, :, at, :],
                dst_ref=far_recv.at[side, pair, :, at, :],
                send_sem=halo_send.at[group, j, side, 1],
                recv_sem=halo_recv.at[group, j, side, 1],
                device_id=device, device_id_type=MESH))
        return copies

    def step_copy(step, j):
        at = pl.ds(j * rows, rows)
        src, dst, device = (
            (resampled.at[0, :, :, at, :], outer_in.at[:, :, at, :], dev_outer),
            (outer_sel.at[:, 1 - half, at, :], inner_in.at[:, at, :], dev_inner),
            (inner_sel.at[:, at, :], cross_in.at[:, at, :], dev_cross),
            (final_own.at[:, at, :], final_in.at[:, at, :], dev_inner),
        )[step]
        return pltpu.make_async_remote_copy(
            src_ref=src, dst_ref=dst,
            send_sem=ref_send.at[step, j], recv_sem=ref_recv.at[step, j],
            device_id=device, device_id_type=MESH)

    def build_band(i):
        phase = phase_ref[order[i]]
        shift = shift_ref[order[i]]
        hot = jnp.where(
            lax.broadcasted_iota(jnp.int32, (PHASES, 512), 0) == phase, 1.0, 0.0).astype(BF16)
        taps = jnp.dot(table_ref[...], hot, preferred_element_type=F32)
        column = lax.broadcasted_iota(jnp.int32, (1, 512), 1)
        first = (column & 255) + shift + 253
        block = first >> 3
        place = lax.broadcasted_iota(jnp.int32, (8, 512), 0) - (first & 7)
        parts = []
        for base in (0, 8):
            now = jnp.zeros((8, 512), F32)
            later = jnp.zeros((8, 512), F32)
            for k in range(TAPS):
                tap = taps[base + k:base + k + 1, :]
                now = jnp.where(place == k, tap, now)
                if k > 0:
                    later = jnp.where(place + 8 == k, tap, later)
            parts.append((now, later))
        outside_left = (column < 256) & (me_r == 0)
        outside_right = (column >= 256) & (me_r == rngs - 1)
        regions = (jnp.where(outside_left, -9, block), block, jnp.where(outside_right, -9, block))
        for region, where_at in enumerate(regions):
            spread = jnp.broadcast_to(where_at, (8, 512))

            def fill(t, carry):
                masks = [spread == 2 * t + u for u in (-1, 0, 1)]
                for (now, later), band in zip(parts, (band_hi, band_lo)):
                    low = jnp.where(masks[1], now, jnp.where(masks[0], later, 0.0))
                    up = jnp.where(masks[2], now, jnp.where(masks[1], later, 0.0))
                    band[i, pl.ds(pl.multiple_of(t * 16, 16), 16), :] = (
                        jnp.concatenate([low, up], axis=0).astype(BF16))
                return carry

            lax.fori_loop(region * 16, region * 16 + 16, fill, 0)

    def resample(i, j):
        at = pl.ds(j * rows, rows)
        centre = two_rows(own[:, order[i], :, at, :])
        near = [two_rows(near_recv[side, i, :, :, at, :]) for side in range(2)]
        packed = [two_rows(far_recv[side, i, :, at, :]) for side in range(2)]
        before = jnp.concatenate([half_turn(packed[0]), packed[0]], axis=0)
        after = jnp.concatenate([packed[1], half_turn(packed[1])], axis=0)
        windows = (
            jnp.concatenate([before, near[0], centre], axis=1),
            jnp.concatenate([centre, near[1], after], axis=1),
        )
        for n, window in enumerate(windows):
            cols = pl.ds(n * 256, 256)
            total = jnp.dot(window, band_hi[i, :, cols], preferred_element_type=F32)
            total += jnp.dot(window, band_lo[i, :, cols], preferred_element_type=F32)
            resampled[i, :, :, at, cols] = total.astype(BF16).reshape(2, 2, rows, 256)

    def looks_of(j):
        at = pl.ds(j * rows, rows)
        group = lax.broadcasted_iota(jnp.int32, (512, 128), 0) // LOOK_RG
        ones = jnp.where(group == lax.broadcasted_iota(jnp.int32, (512, 128), 1), 1.0, 0.0).astype(BF16)

        def summed(v, row):
            high = v.astype(BF16)
            low = (v - high.astype(F32)).astype(BF16)
            lane_sums[row * rows:(row + 1) * rows, :] = (
                jnp.dot(high, ones, preferred_element_type=F32)
                + jnp.dot(low, ones, preferred_element_type=F32))

        out_rows = rows // LOOK_AZ
        for which, b_ref in ((half, final_own), (1 - half, final_in)):
            b_re, b_im = b_ref[0, at, :].astype(F32), b_ref[1, at, :].astype(F32)
            summed(b_re * b_re + b_im * b_im, 12)
            for i in range(4):
                a_re = resampled[i, 0, which, at, :].astype(F32)
                a_im = resampled[i, 1, which, at, :].astype(F32)
                summed(a_re * b_re + a_im * b_im, 3 * i)
                summed(a_im * b_re - a_re * b_im, 3 * i + 1)
                summed(a_re * a_re + a_im * a_im, 3 * i + 2)
            patches = sum(
                lane_sums[pl.ds(k, 13 * out_rows, stride=LOOK_AZ), :] for k in range(LOOK_AZ))
            sum_b = patches[12 * out_rows:13 * out_rows]
            to = pl.ds(j * out_rows, out_rows)
            for i in range(4):
                s_re, s_im, s_a = (
                    patches[(3 * i + u) * out_rows:(3 * i + u + 1) * out_rows] for u in range(3))
                looks[i, 0, which, to, :] = s_re / (LOOK_AZ * LOOK_RG)
                looks[i, 1, which, to, :] = s_im / (LOOK_AZ * LOOK_RG)
                looks[i, 2, which, to, :] = (
                    jnp.sqrt(s_re * s_re + s_im * s_im) / jnp.sqrt(s_a * sum_b + 1e-06))

    load.wait()
    stage(0)
    stage(1)
    pl.semaphore_wait(barrier, 5)
    started = []
    for j in range(chunks):
        for copy in halo(0, j):
            copy.start()
            started.append(copy)
    build_band(0)
    build_band(1)
    stage(2)
    stage(3)

    for t in range(chunks + 4):
        if t < chunks:
            for copy in halo(0, t):
                copy.wait_recv()
            resample(0, t)
            copy = step_copy(0, t)
            copy.start()
            started.append(copy)
            resample(1, t)
        if t == 0:
            for j in range(chunks):
                for copy in halo(1, j):
                    copy.start()
                    started.append(copy)
        if 0 <= t - 1 < chunks:
            j = t - 1
            at = pl.ds(j * rows, rows)
            step_copy(0, j).wait_recv()
            outer_sel[:, :, at, :] = lax.select(
                owner_x == outer_x, outer_in[:, :, at, :], resampled[mine_at, :, :, at, :])
            copy = step_copy(1, j)
            copy.start()
            started.append(copy)
        if 0 <= t - 2 < chunks:
            j = t - 2
            at = pl.ds(j * rows, rows)
            step_copy(1, j).wait_recv()
            inner_sel[:, at, :] = lax.select(
                (owner_x == inner_x) | (owner_x == 3 - inner_x),
                inner_in[:, at, :], outer_sel[:, half, at, :])
            copy = step_copy(2, j)
            copy.start()
            started.append(copy)
        if 0 <= t - 3 < chunks:
            j = t - 3
            at = pl.ds(j * rows, rows)
            step_copy(2, j).wait_recv()
            final_own[:, at, :] = lax.select(
                owner_yh == yh, inner_sel[:, at, :], cross_in[:, at, :])
            copy = step_copy(3, j)
            copy.start()
            started.append(copy)
        if t == 1:
            build_band(2)
            build_band(3)
        if 0 <= t - 4 < chunks:
            j = t - 4
            for copy in halo(1, j):
                copy.wait_recv()
            resample(2, j)
            resample(3, j)
            step_copy(3, j).wait_recv()
            looks_of(j)
    for d in range(4):
        at = jnp.where(p0 == d, 0, jnp.where(p1 == d, 1, jnp.where(p2 == d, 2, 3)))
        ml_ref[0, d] = looks[at, 0, :, :, 0:32]
        ml_ref[1, d] = looks[at, 1, :, :, 0:32]
        coh_ref[d] = looks[at, 2, :, :, 0:32]
    for copy in started:
        copy.wait_send()


def on_device(slc, shift_table, phase_table, reference_ids):
    dates_dev, lines = slc.shape[1], slc.shape[2]
    half_lines = lines // 2
    chunks = min(CHUNKS, half_lines // 32)
    rows = half_lines // chunks
    dates, rngs = lax.axis_size("date"), lax.axis_size("rng")
    out_half = half_lines // LOOK_AZ
    vmem = pl.BlockSpec(memory_space=pltpu.VMEM)
    multilook, coherence = pl.pallas_call(
        functools.partial(kernel, dates, rngs, chunks, half_lines),
        out_shape=(
            jax.ShapeDtypeStruct((2, 4, 2, out_half, 32), F32),
            jax.ShapeDtypeStruct((4, 2, out_half, 32), F32),
        ),
        in_specs=[pl.BlockSpec(memory_space=pltpu.SMEM), vmem, vmem, vmem,
                  pl.BlockSpec(memory_space=pl.ANY)],
        out_specs=(vmem, vmem),
        scratch_shapes=[
            pltpu.VMEM((2, 4, 2, half_lines, 512), BF16),
            pltpu.VMEM((2, 4, 2, 2, half_lines, 128), BF16),
            pltpu.VMEM((2, 4, 2, half_lines, 128), BF16),
            pltpu.VMEM((2, 4, 2, 2, half_lines, 128), BF16),
            pltpu.VMEM((2, 4, 2, half_lines, 128), BF16),
            pltpu.VMEM((4, WIN, 512), BF16),
            pltpu.VMEM((4, WIN, 512), BF16),
            pltpu.VMEM((4, 2, 2, half_lines, 512), BF16),
            pltpu.VMEM((2, 2, half_lines, 512), BF16),
            pltpu.VMEM((2, 2, half_lines, 512), BF16),
            pltpu.VMEM((2, half_lines, 512), BF16),
            pltpu.VMEM((2, half_lines, 512), BF16),
            pltpu.VMEM((2, half_lines, 512), BF16),
            pltpu.VMEM((2, half_lines, 512), BF16),
            pltpu.VMEM((2, half_lines, 512), BF16),
            pltpu.VMEM((13 * rows, 128), F32),
            pltpu.VMEM((4, 3, 2, out_half, 128), F32),
            pltpu.SemaphoreType.DMA,
            pltpu.SemaphoreType.DMA((2, chunks, 2, 2)),
            pltpu.SemaphoreType.DMA((2, chunks, 2, 2)),
            pltpu.SemaphoreType.DMA((4, chunks)),
            pltpu.SemaphoreType.DMA((4, chunks)),
        ],
        compiler_params=pltpu.CompilerParams(
            collective_id=0, has_side_effects=True, vmem_limit_bytes=48 * 1024 * 1024),
    )(
        reference_ids,
        shift_table.reshape(4, 1, 512),
        phase_table.reshape(4, 1, 512),
        tap_table(),
        slc.reshape(2, dates_dev, 2, half_lines, 512),
    )
    return multilook.reshape(2, 4, 2 * out_half, 32), coherence.reshape(4, 2 * out_half, 32)


def solution(mesh):
    placed = (P(None, "date", None, "rng"), P("date", "rng"), P("date", "rng"), P())
    return jax.shard_map(
        on_device,
        mesh=mesh,
        in_specs=placed,
        out_specs=(P(None, "date", None, "rng"), P("date", None, "rng")),
        check_vma=False,
    )
```

time: 306 us -> 47.3 us (0.15)
  waiting for transfers between devices: 193 us -> 0 us
  Pallas kernels: 0 us -> 40.1 us
  local copies, waits for them, and re-layouts: 39.1 us -> 5.85 us
  other arithmetic: 31.5 us -> 0 us
  matrix products: 15.4 us -> 0 us
  between operations: 14.2 us -> 0.64 us
  starting transfers between devices: 5.6 us -> 0 us
  loops' own time: 5.08 us -> 0 us
    psum x2 -> x0, waiting for transfers between devices: 180 us -> none  [from_root(): return lax.psum(block, axis)]
    pallas_call x0 -> x1, Pallas kernels: none -> 40.1 us  [on_device(): pl.pallas_call(functools.partial(kernel, dates, rngs, chunks, half_lines)...]
    reduce_sum x3 -> x0, other arithmetic: 20.6 us -> none  [the longest x2 20.5 us: patch_sum(): v.reshape(n, lines // LOOK_AZ, LOOK_AZ, pixels // LOOK_RG, LOOK_RG)]
    convert_element_type x2 -> x0, local copies, waits for them, and re-layouts: 19.7 us -> none  [the longest x1 10.8 us: patch_stats(): date_re = dates[0].astype(jnp.float32)]
    dot_general x8 -> x0, matrix products: 15.4 us -> none  [the longest x4 14.1 us: resample_window(): summed = jnp.dot(flat, band, precision=lax.Precision.HIGHEST)]
    ppermute x2 -> x0, waiting for transfers between devices: 13.3 us -> none  [the longest x1 13.3 us: extended(): before = lax.ppermute(last, axis, up)]
    mul x2 -> x0, local copies, waits for them, and re-layouts: 5.57 us -> none  [patch_stats(): ifg_re = date_re * ref_re + date_im * ref_im]
    ppermute x2 -> x0, starting transfers between devices: 5.55 us -> none  [the longest x1 3.63 us: extended(): after = lax.ppermute(leading, axis, down)]
  transfers between devices with their start and end apart: 4 -> 0, of which waited for: 3 -> 0; matrix products, arithmetic and copies ran while one was open for 2% -> 0% of each run, Pallas kernels for 0% -> 0%
where the time goes in v1:
time: 47.3 us; the launch traced here: 46.6 us
  Pallas kernels  40.1 us (85%)
  local copies, waits for them, and re-layouts  5.85 us (12%)
  between operations  0.64 us (1%)
    pallas_call x1, Pallas kernels, on_device(): pl.pallas_call(functools.partial(kernel, dates, rngs, chunks, half_lines)...  40.1 us
    unnamed x8, local copies, waits for them, and re-layouts  4.44 us

profile of v1, /device:TPU:8, one launch (start us, length us, event | category | flops | bytes accessed | tf_op | source)
XLA Modules:
  0.0 46.6 jit_solution(7484543876643735089)
XLA Ops:
  0.6 0.7 %reshape.19.shift_ref = s32[4,1,512]{2,1,0:T(1,128)S(1)} reshape(s32[4,512]{1,0:T(4,128)} %param.6) | data formatting | bytes 16384 | tf_op jit(solution)/shard_map/reshape | solution.py:337
  1.3 0.7 %reshape.20.phase_ref = s32[4,1,512]{2,1,0:T(1,128)S(1)} reshape(s32[4,512]{1,0:T(4,128)} %param.7) | data formatting | bytes 16384 | tf_op jit(solution)/shard_map/reshape | solution.py:338
  2.0 0.0 copy-start
  2.0 1.6 %copy-done = bf16[2,4,256,512]{3,2,1,0:T(8,128)(2,1)S(1)} copy-done((bf16[2,4,256,512]{3,2,1,0:T(8,128)(2,1)S(1)}, bf16[2,4,256,512]{3,2,1,0:T(8,128)(2,1)}, u32[]{:S(2)}) %copy-start) | copy-done | bytes 2097176
  3.6 0.0 copy-start.1
  3.6 0.7 %copy-done.1 = bf16[16,256]{1,0:T(8,128)(2,1)S(1)} copy-done((bf16[16,256]{1,0:T(8,128)(2,1)S(1)}, bf16[16,256]{1,0:T(8,128)(2,1)}, u32[]{:S(2)}) %copy-start.1) | copy-done | bytes 8216
  4.3 0.0 copy-start.2
  4.3 0.7 %copy-done.2 = s32[2]{0:T(128)S(1)} copy-done((s32[2]{0:T(128)S(1)}, s32[2]{0:T(128)}, u32[]{:S(2)}) %copy-start.2) | copy-done | bytes 32
  5.0 40.1 %shard_map.68 = (f32[2,4,2,32,32]{4,3,2,1,0:T(8,128)S(1)}, f32[4,2,32,32]{3,2,1,0:T(8,128)S(1)}) custom-call(s32[2]{0:T(128)S(1)} %copy-done.2, s32[4,1,512]{2,1,0:T(1,128)S(1)} %reshape.19.shift_ref, s32[4,1,512]{2,1,0:T(1,128)S(1)} %reshape.20.phase_ref, bf16[16,256]{1,0:T(8,128)(2,1)S(1)} %copy-done.1, bf16[2,4,2,128,512]{4,3,2,1,0:T(8,128)(2,1)S(1)} %bitcast.3), custom_call_target="tpu_custom_call" | custom-call | tf_op jit(solution)/shard_map/pallas_call | solution.py:300
  45.1 0.8 %copy.7 = f32[2,4,64,32]{2,3,1,0:T(8,128)} copy(f32[2,4,64,32]{3,2,1,0:T(8,128)S(1)} %bitcast.4) | data formatting | bytes 131072
  45.9 0.7 %copy.8 = f32[4,64,32]{1,2,0:T(8,128)} copy(f32[4,64,32]{2,1,0:T(8,128)S(1)} %bitcast.5) | data formatting | bytes 65536
Async XLA Ops:
  2.0 1.6 %copy-start = (bf16[2,4,256,512]{3,2,1,0:T(8,128)(2,1)S(1)}, bf16[2,4,256,512]{3,2,1,0:T(8,128)(2,1)}, u32[]{:S(2)}) copy-start(bf16[2,4,256,512]{3,2,1,0:T(8,128)(2,1)} %param.5) | copy-start | bytes 6291460
  3.6 0.7 %copy-start.1 = (bf16[16,256]{1,0:T(8,128)(2,1)S(1)}, bf16[16,256]{1,0:T(8,128)(2,1)}, u32[]{:S(2)}) copy-start(bf16[16,256]{1,0:T(8,128)(2,1)} %constant.10.table_ref) | copy-start | bytes 24580
  4.3 0.7 %copy-start.2 = (s32[2]{0:T(128)S(1)}, s32[2]{0:T(128)}, u32[]{:S(2)}) copy-start(s32[2]{0:T(128)} %ids.1) | copy-start | bytes 28

commit v2 on v1

v2 whole, which is shorter than its diff:
```python
import functools

import jax
import jax.numpy as jnp
import numpy as np
from jax import lax
from jax.experimental import pallas as pl
from jax.experimental.pallas import tpu as pltpu
from jax.sharding import PartitionSpec as P

TAPS = 8
PHASES = 256
LOOK_AZ = 4
LOOK_RG = 16
CHUNKS = 4
WIN = 768
MESH = pl.DeviceIdType.MESH
BF16 = jnp.bfloat16
F32 = jnp.float32


def tap_table():
    fraction = np.arange(PHASES) / PHASES
    tap_offset = np.arange(TAPS) - (TAPS // 2 - 1)
    t = tap_offset[:, None] - fraction[None, :]
    weight = np.sinc(t) * (0.5 + 0.5 * np.cos(np.pi * t / (TAPS // 2 + 1)))
    weight = jnp.asarray(weight / weight.sum(axis=0, keepdims=True), F32)
    high = weight.astype(BF16)
    low = (weight - high.astype(F32)).astype(BF16)
    return jnp.concatenate([high, low], axis=0)


def half_turn(v):
    return pltpu.roll(v.astype(F32), 64, 1).astype(BF16)


def two_rows(v):
    return v.reshape(-1, v.shape[-1])


def kernel(
    dates, rngs, chunks, half_lines,
    ids_hbm, shift_hbm, phase_hbm, table_hbm, slc_hbm,
    out_ref,
    ids, shift_ref, phase_ref, table_ref,
    own, edge_out, edge_in, band_hi, band_lo,
    resampled, offers, mine_out, merged, cross_in, final,
    lane_sums, power_b, looks, turned,
    own_sem, halo_send, halo_recv, ref_send, ref_recv,
):
    rows = half_lines // chunks
    me_d, me_r = lax.axis_index("date"), lax.axis_index("rng")
    x, yh = me_d // 2, me_d % 2
    outer_x = 3 - x
    inner_x = x + 1 - 2 * (x % 2)
    far_x = 3 - inner_x
    half = x % 2
    left, right = (me_r + rngs - 1) % rngs, (me_r + 1) % rngs
    stack = x // 2
    dev_outer = (outer_x * 2 + yh, me_r)
    dev_inner = (inner_x * 2 + yh, me_r)
    dev_far = (far_x * 2 + yh, me_r)
    dev_cross = (x * 2 + 1 - yh, me_r)
    dev_left, dev_right = (me_d, left), (me_d, right)

    loads = [
        pltpu.make_async_copy(src, dst, own_sem.at[i])
        for i, (src, dst) in enumerate((
            (ids_hbm, ids), (slc_hbm, own), (shift_hbm, shift_ref),
            (phase_hbm, phase_ref), (table_hbm, table_ref)))
    ]
    for copy in loads:
        copy.start()
    barrier = pltpu.get_barrier_semaphore()
    for device in (dev_left, dev_right, dev_outer, dev_far, dev_inner, dev_cross):
        pl.semaphore_signal(barrier, inc=1, device_id=device, device_id_type=MESH)
    loads[0].wait()

    mine = jnp.where(stack == 0, ids[0], ids[1])
    other = jnp.where(stack == 0, ids[1], ids[0])
    slot_m, slot_o = mine % 4, other % 4
    p0 = slot_o
    same = slot_m == slot_o
    p1 = jnp.where(same, (slot_o + 1) % 4, slot_m)
    p2 = jnp.where((p0 != 0) & (p1 != 0), 0, jnp.where((p0 != 1) & (p1 != 1), 1, 2))
    p3 = 6 - p0 - p1 - p2
    order = (p0, p1, p2, p3)
    mine_at = jnp.where(same, 0, 1)
    owner = mine // 4
    owner_x, owner_yh = owner // 2, owner % 2

    lane = lax.broadcasted_iota(jnp.int32, (1, 128), 1)
    started = []

    def stage(i):
        for re_im in range(2):
            edge_out[0, i, re_im] = own[re_im, order[i], :, :, 384:512]
            edge_out[1, i, re_im] = own[re_im, order[i], :, :, 0:128]
        for h in range(2):
            re = own[0, order[i], h, :, 256:384].astype(F32)
            im = own[1, order[i], h, :, 256:384].astype(F32)
            edge_out[0, i, 2, h] = jnp.where(lane < 64, pltpu.roll(re, 64, 1), im).astype(BF16)
            re = own[0, order[i], h, :, 128:256].astype(F32)
            im = own[1, order[i], h, :, 128:256].astype(F32)
            edge_out[1, i, 2, h] = jnp.where(lane < 64, re, pltpu.roll(im, 64, 1)).astype(BF16)

    def halo(i, j):
        at = pl.ds(j * rows, rows)
        return [
            pltpu.make_async_remote_copy(
                src_ref=edge_out.at[side, i, :, :, at, :],
                dst_ref=edge_in.at[side, i, :, :, at, :],
                send_sem=halo_send.at[i, j, side],
                recv_sem=halo_recv.at[i, j, side],
                device_id=device, device_id_type=MESH)
            for side, device in enumerate((dev_right, dev_left))
        ]

    def send_halo(i, j):
        for copy in halo(i, j):
            copy.start()
            started.append(copy)

    def step_copy(step, j):
        at = pl.ds(j * rows, rows)
        src, dst, device = (
            (resampled.at[0, :, 1 - half, at, :], offers.at[0, :, at, :], dev_outer),
            (resampled.at[0, :, half, at, :], offers.at[1, :, at, :], dev_far),
            (mine_out.at[:, at, :], offers.at[2, :, at, :], dev_inner),
            (merged.at[:, at, :], cross_in.at[:, at, :], dev_cross),
            (final.at[:, half, at, :], final.at[:, half, at, :], dev_inner),
        )[step]
        return pltpu.make_async_remote_copy(
            src_ref=src, dst_ref=dst,
            send_sem=ref_send.at[step, j], recv_sem=ref_recv.at[step, j],
            device_id=device, device_id_type=MESH)

    def send_step(step, j):
        copy = step_copy(step, j)
        copy.start()
        started.append(copy)

    def build_band(i):
        phase = phase_ref[pl.ds(order[i], 1), :]
        shift = shift_ref[pl.ds(order[i], 1), :]
        hot = jnp.where(
            lax.broadcasted_iota(jnp.int32, (PHASES, 512), 0) == phase, 1.0, 0.0).astype(BF16)
        taps = jnp.dot(table_ref[...], hot, preferred_element_type=F32)
        column = lax.broadcasted_iota(jnp.int32, (1, 512), 1)
        first = (column & 255) + shift + 253
        block = first >> 3
        place = lax.broadcasted_iota(jnp.int32, (8, 512), 0) - (first & 7)
        parts = []
        for base in (0, 8):
            now = jnp.zeros((8, 512), F32)
            later = jnp.zeros((8, 512), F32)
            for k in range(TAPS):
                tap = taps[base + k:base + k + 1, :]
                now = jnp.where(place == k, tap, now)
                if k > 0:
                    later = jnp.where(place + 8 == k, tap, later)
            parts.append((now, later))
        outside_left = (column < 256) & (me_r == 0)
        outside_right = (column >= 256) & (me_r == rngs - 1)
        regions = (jnp.where(outside_left, -9, block), block, jnp.where(outside_right, -9, block))
        for region, where_at in enumerate(regions):
            spread = jnp.broadcast_to(where_at, (8, 512))

            def fill(t, carry):
                masks = [spread == 2 * t + u for u in (-1, 0, 1)]
                for (now, later), band in zip(parts, (band_hi, band_lo)):
                    low = jnp.where(masks[1], now, jnp.where(masks[0], later, 0.0))
                    up = jnp.where(masks[2], now, jnp.where(masks[1], later, 0.0))
                    band[i, pl.ds(pl.multiple_of(t * 16, 16), 16), :] = (
                        jnp.concatenate([low, up], axis=0).astype(BF16))
                return carry

            lax.fori_loop(region * 16, region * 16 + 16, fill, 0)

    def arrive(i, j):
        for copy in halo(i, j):
            copy.wait_recv()

    def resample(i, j):
        size = half_lines if j is None else rows
        at = pl.ds(0 if j is None else j * rows, size)
        centre = two_rows(own[:, order[i], :, at, :])
        near = [two_rows(edge_in[side, i, 0:2, :, at, :]) for side in range(2)]
        packed = [two_rows(edge_in[side, i, 2, :, at, :]) for side in range(2)]
        before = jnp.concatenate([half_turn(packed[0]), packed[0]], axis=0)
        after = jnp.concatenate([packed[1], half_turn(packed[1])], axis=0)
        windows = (
            jnp.concatenate([before, near[0], centre], axis=1),
            jnp.concatenate([centre, near[1], after], axis=1),
        )
        for n, window in enumerate(windows):
            cols = pl.ds(n * 256, 256)
            total = jnp.dot(window, band_hi[i, :, cols], preferred_element_type=F32)
            total += jnp.dot(window, band_lo[i, :, cols], preferred_element_type=F32)
            resampled[i, :, :, at, cols] = total.astype(BF16).reshape(2, 2, size, 256)

    def offer_other(j):
        arrive(0, j)
        resample(0, j)
        send_step(0, j)
        send_step(1, j)

    def offer_mine(j):
        arrive(1, j)
        resample(1, j)
        at = pl.ds(j * rows, rows)
        mine_out[:, at, :] = resampled[mine_at, :, 1 - half, at, :]
        send_step(2, j)

    def merge(j):
        at = pl.ds(j * rows, rows)
        for step in range(3):
            step_copy(step, j).wait_recv()
        found = lax.select(owner_x == outer_x, offers[0, :, at, :], resampled[mine_at, :, half, at, :])
        found = lax.select(owner_x == far_x, offers[1, :, at, :], found)
        merged[:, at, :] = lax.select(owner_x == inner_x, offers[2, :, at, :], found)
        send_step(3, j)

    def cross(j):
        at = pl.ds(j * rows, rows)
        step_copy(3, j).wait_recv()
        final[:, half, at, :] = lax.select(owner_yh == yh, merged[:, at, :], cross_in[:, at, :])
        send_step(4, j)

    group = lax.broadcasted_iota(jnp.int32, (512, 128), 0) // LOOK_RG
    ones = jnp.where(group == lax.broadcasted_iota(jnp.int32, (512, 128), 1), 1.0, 0.0).astype(BF16)

    def patch_sums(parts):
        count = 2 * rows * len(parts)
        whole = jnp.concatenate(parts, axis=0)
        high = whole.astype(BF16)
        low = (whole - high.astype(F32)).astype(BF16)
        lane_sums[0:count, :] = (
            jnp.dot(high, ones, preferred_element_type=F32)
            + jnp.dot(low, ones, preferred_element_type=F32))
        found = sum(lane_sums[pl.ds(k, count // LOOK_AZ, stride=LOOK_AZ), :] for k in range(LOOK_AZ))
        each = 2 * rows // LOOK_AZ
        return [found[u * each:(u + 1) * each] for u in range(len(parts))]

    def reference_tile(j):
        at = pl.ds(j * rows, rows)
        return [two_rows(final[u, :, at, :]).astype(F32) for u in range(2)]

    def reference_power(j):
        step_copy(4, j).wait_recv()
        b_re, b_im = reference_tile(j)
        power_b[j], = patch_sums([b_re * b_re + b_im * b_im])

    def look(i, j):
        at = pl.ds(j * rows, rows)
        b_re, b_im = reference_tile(j)
        a_re, a_im = (two_rows(resampled[i, u, :, at, :]).astype(F32) for u in range(2))
        s_re, s_im, s_a = patch_sums(
            [a_re * b_re + a_im * b_im, a_im * b_re - a_re * b_im, a_re * a_re + a_im * a_im])
        coherence = jnp.sqrt(s_re * s_re + s_im * s_im) / jnp.sqrt(s_a * power_b[j] + 1e-06)
        out_rows = rows // LOOK_AZ
        to = pl.ds(j * out_rows, out_rows)
        scale = 1.0 / (LOOK_AZ * LOOK_RG)
        for u, v in enumerate((s_re * scale, s_im * scale, coherence)):
            looks[i, u, :, to, :] = v.reshape(2, out_rows, 128)

    def turn(i):
        for u in range(3):
            turned[i, u] = two_rows(looks[i, u]).T[0:32, :]

    loads[1].wait()
    stage(0)
    pl.semaphore_wait(barrier, 6)
    for j in range(chunks):
        send_halo(0, j)
    stage(1)
    for j in range(chunks):
        send_halo(1, j)
    for copy in loads[2:]:
        copy.wait()
    build_band(0)
    build_band(1)
    for j in range(chunks):
        offer_other(j)
    for i in (2, 3):
        stage(i)
        for j in range(chunks):
            send_halo(i, j)
    for j in range(chunks):
        offer_mine(j)
    build_band(2)
    build_band(3)

    def whole(i):
        for j in range(chunks):
            arrive(i, j)
        resample(i, None)

    def looks_at(j, dates_now):
        for i in dates_now:
            look(i, j)

    merge(0)
    merge(1)
    cross(0)
    merge(2)
    whole(2)
    cross(1)
    merge(3)
    reference_power(0)
    looks_at(0, (0, 1, 2))
    cross(2)
    reference_power(1)
    looks_at(1, (0, 1, 2))
    cross(3)
    whole(3)
    reference_power(2)
    looks_at(2, (0, 1, 2, 3))
    looks_at(0, (3,))
    looks_at(1, (3,))
    reference_power(3)
    looks_at(3, (0, 1, 2, 3))
    for i in range(4):
        turn(i)
    for d in range(4):
        at = jnp.where(p0 == d, 0, jnp.where(p1 == d, 1, jnp.where(p2 == d, 2, 3)))
        for u in range(3):
            out_ref[u, d] = turned[at, u]
    for copy in started:
        copy.wait_send()


def hand_out(found_ref, ml_ref, coh_ref, sems):
    ml_ref[...] = found_ref[0:2]
    coh_ref[...] = found_ref[2]


def on_device(slc, shift_table, phase_table, reference_ids):
    dates_dev, lines = slc.shape[1], slc.shape[2]
    half_lines = lines // 2
    chunks = min(CHUNKS, half_lines // 32)
    rows = half_lines // chunks
    dates, rngs = lax.axis_size("date"), lax.axis_size("rng")
    out_half = half_lines // LOOK_AZ
    vmem = pl.BlockSpec(memory_space=pltpu.VMEM)
    found = pl.pallas_call(
        functools.partial(kernel, dates, rngs, chunks, half_lines),
        out_shape=jax.ShapeDtypeStruct((3, 4, 32, 2 * out_half), F32),
        in_specs=[pl.BlockSpec(memory_space=pl.ANY)] * 5,
        out_specs=vmem,
        scratch_shapes=[
            pltpu.SMEM((2,), jnp.int32),
            pltpu.VMEM((4, 512), jnp.int32),
            pltpu.VMEM((4, 512), jnp.int32),
            pltpu.VMEM((2 * TAPS, PHASES), BF16),
            pltpu.VMEM((2, 4, 2, half_lines, 512), BF16),
            pltpu.VMEM((2, 4, 3, 2, half_lines, 128), BF16),
            pltpu.VMEM((2, 4, 3, 2, half_lines, 128), BF16),
            pltpu.VMEM((4, WIN, 512), BF16),
            pltpu.VMEM((4, WIN, 512), BF16),
            pltpu.VMEM((4, 2, 2, half_lines, 512), BF16),
            pltpu.VMEM((3, 2, half_lines, 512), BF16),
            pltpu.VMEM((2, half_lines, 512), BF16),
            pltpu.VMEM((2, half_lines, 512), BF16),
            pltpu.VMEM((2, half_lines, 512), BF16),
            pltpu.VMEM((2, 2, half_lines, 512), BF16),
            pltpu.VMEM((6 * rows, 128), F32),
            pltpu.VMEM((chunks, 2 * rows // LOOK_AZ, 128), F32),
            pltpu.VMEM((4, 3, 2, out_half, 128), F32),
            pltpu.VMEM((4, 3, 32, 2 * out_half), F32),
            pltpu.SemaphoreType.DMA((5,)),
            pltpu.SemaphoreType.DMA((4, chunks, 2)),
            pltpu.SemaphoreType.DMA((4, chunks, 2)),
            pltpu.SemaphoreType.DMA((5, chunks)),
            pltpu.SemaphoreType.DMA((5, chunks)),
        ],
        compiler_params=pltpu.CompilerParams(
            collective_id=0, has_side_effects=True, vmem_limit_bytes=62 * 1024 * 1024),
    )(
        reference_ids,
        shift_table,
        phase_table,
        tap_table(),
        slc.reshape(2, dates_dev, 2, half_lines, 512),
    )
    anywhere = pl.BlockSpec(memory_space=pl.ANY)
    multilook, coherence = pl.pallas_call(
        hand_out,
        out_shape=(
            jax.ShapeDtypeStruct((2, 4, 32, 2 * out_half), F32),
            jax.ShapeDtypeStruct((4, 32, 2 * out_half), F32),
        ),
        in_specs=[vmem],
        out_specs=(vmem, vmem),
        scratch_shapes=[pltpu.SemaphoreType.DMA((2,))],
    )(found)
    return jnp.swapaxes(multilook, 2, 3), jnp.swapaxes(coherence, 1, 2)


def solution(mesh):
    placed = (P(None, "date", None, "rng"), P("date", "rng"), P("date", "rng"), P())
    return jax.shard_map(
        on_device,
        mesh=mesh,
        in_specs=placed,
        out_specs=(P(None, "date", None, "rng"), P("date", None, "rng")),
        check_vma=False,
    )
```

time: 47.3 us -> 40.7 us (0.86); the launches traced: 46.6 us -> 40.5 us
  local copies, waits for them, and re-layouts: 5.85 us -> 0 us
    unnamed x8 -> x0, local copies, waits for them, and re-layouts: 4.44 us -> none
    pallas_call x1, Pallas kernels: 40.1 us -> 38.3 us  [on_device(): pl.pallas_call(functools.partial(kernel, dates, rngs, chunks, half_lines)...]
    pallas_call x0 -> x1, Pallas kernels: none -> 1.63 us  [on_device(): pl.pallas_call(hand_out, out_shape=(jax.ShapeDtypeStruct((2, 4, 32, 2 * o...]
    reshape x2 -> x0, local copies, waits for them, and re-layouts: 1.41 us -> none  [the longest x1 0.7 us: on_device(): shift_table.reshape(4, 1, 512)]
where the time goes in v2:
time: 40.7 us; the launch traced here: 40.5 us
  Pallas kernels  39.9 us (98%)
  between operations  0.64 us (2%)
    pallas_call x1, Pallas kernels, on_device(): pl.pallas_call(functools.partial(kernel, dates, rngs, chunks, half_lines)...  38.3 us
    pallas_call x1, Pallas kernels, on_device(): pl.pallas_call(hand_out, out_shape=(jax.ShapeDtypeStruct((2, 4, 32, 2 * o...  1.63 us

profile of v2, /device:TPU:8, one launch (start us, length us, event | category | flops | bytes accessed | tf_op | source)
XLA Modules:
  0.0 40.5 jit_solution(8885482628279714880)
XLA Ops:
  0.6 38.3 %shard_map.68.found_ref = f32[3,4,32,64]{3,2,1,0:T(8,128)} custom-call(s32[2]{0:T(128)} %ids_hbm.1, s32[4,512]{1,0:T(4,128)} %shift_hbm.1, s32[4,512]{1,0:T(4,128)} %phase_hbm.1, bf16[16,256]{1,0:T(8,128)(2,1)} %constant.10.table_hbm, bf16[2,4,2,128,512]{4,3,2,1,0:T(8,128)(2,1)} %bitcast.3), custom_call_target="tpu_custom_call" | custom-call | tf_op jit(solution)/shard_map/pallas_call | solution.py:346
  38.9 1.6 %shard_map.69 = (f32[2,4,32,64]{3,2,1,0:T(8,128)}, f32[4,32,64]{2,1,0:T(8,128)}) custom-call(f32[3,4,32,64]{3,2,1,0:T(8,128)} %shard_map.68.found_ref), custom_call_target="tpu_custom_call" | custom-call | tf_op jit(solution)/shard_map/pallas_call | solution.py:387

commit v3 on v2

--- a/solution.py
+++ b/solution.py
@@ -12,7 +12,7 @@
 PHASES = 256
 LOOK_AZ = 4
 LOOK_RG = 16
-CHUNKS = 4
+CHUNKS = (32, 48, 32, 16)
 WIN = 768
 MESH = pl.DeviceIdType.MESH
 BF16 = jnp.bfloat16
@@ -39,7 +39,7 @@
 
 
 def kernel(
-    dates, rngs, chunks, half_lines,
+    dates, rngs, sizes, blocks, half_lines,
     ids_hbm, shift_hbm, phase_hbm, table_hbm, slc_hbm,
     out_ref,
     ids, shift_ref, phase_ref, table_ref,
@@ -48,7 +48,10 @@
     lane_sums, power_b, looks, turned,
     own_sem, halo_send, halo_recv, ref_send, ref_recv,
 ):
-    rows = half_lines // chunks
+    rows = half_lines // blocks
+    chunks = len(sizes)
+    starts = [sum(sizes[:j]) for j in range(chunks)]
+    pieces = (chunks, chunks, 1, 1)
     me_d, me_r = lax.axis_index("date"), lax.axis_index("rng")
     x, yh = me_d // 2, me_d % 2
     outer_x = 3 - x
@@ -63,6 +66,9 @@
     dev_cross = (x * 2 + 1 - yh, me_r)
     dev_left, dev_right = (me_d, left), (me_d, right)
 
+    barrier = pltpu.get_barrier_semaphore()
+    for device in (dev_left, dev_right, dev_outer, dev_far, dev_inner, dev_cross):
+        pl.semaphore_signal(barrier, inc=1, device_id=device, device_id_type=MESH)
     loads = [
         pltpu.make_async_copy(src, dst, own_sem.at[i])
         for i, (src, dst) in enumerate((
@@ -71,9 +77,6 @@
     ]
     for copy in loads:
         copy.start()
-    barrier = pltpu.get_barrier_semaphore()
-    for device in (dev_left, dev_right, dev_outer, dev_far, dev_inner, dev_cross):
-        pl.semaphore_signal(barrier, inc=1, device_id=device, device_id_type=MESH)
     loads[0].wait()
 
     mine = jnp.where(stack == 0, ids[0], ids[1])
@@ -91,6 +94,7 @@
 
     lane = lax.broadcasted_iota(jnp.int32, (1, 128), 1)
     started = []
+    landed = list(range(chunks))
 
     def stage(i):
         for re_im in range(2):
@@ -104,8 +108,11 @@
             im = own[1, order[i], h, :, 128:256].astype(F32)
             edge_out[1, i, 2, h] = jnp.where(lane < 64, re, pltpu.roll(im, 64, 1)).astype(BF16)
 
+    def lines_of(j):
+        return pl.ds(starts[j], sizes[j])
+
     def halo(i, j):
-        at = pl.ds(j * rows, rows)
+        at = lines_of(j) if i < 2 else pl.ds(0, half_lines)
         return [
             pltpu.make_async_remote_copy(
                 src_ref=edge_out.at[side, i, :, :, at, :],
@@ -122,7 +129,7 @@
             started.append(copy)
 
     def step_copy(step, j):
-        at = pl.ds(j * rows, rows)
+        at = lines_of(j)
         src, dst, device = (
             (resampled.at[0, :, 1 - half, at, :], offers.at[0, :, at, :], dev_outer),
             (resampled.at[0, :, half, at, :], offers.at[1, :, at, :], dev_far),
@@ -182,8 +189,8 @@
             copy.wait_recv()
 
     def resample(i, j):
-        size = half_lines if j is None else rows
-        at = pl.ds(0 if j is None else j * rows, size)
+        size = half_lines if j is None else sizes[j]
+        at = pl.ds(0, half_lines) if j is None else lines_of(j)
         centre = two_rows(own[:, order[i], :, at, :])
         near = [two_rows(edge_in[side, i, 0:2, :, at, :]) for side in range(2)]
         packed = [two_rows(edge_in[side, i, 2, :, at, :]) for side in range(2)]
@@ -208,12 +215,12 @@
     def offer_mine(j):
         arrive(1, j)
         resample(1, j)
-        at = pl.ds(j * rows, rows)
+        at = lines_of(j)
         mine_out[:, at, :] = resampled[mine_at, :, 1 - half, at, :]
         send_step(2, j)
 
     def merge(j):
-        at = pl.ds(j * rows, rows)
+        at = lines_of(j)
         for step in range(3):
             step_copy(step, j).wait_recv()
         found = lax.select(owner_x == outer_x, offers[0, :, at, :], resampled[mine_at, :, half, at, :])
@@ -222,7 +229,7 @@
         send_step(3, j)
 
     def cross(j):
-        at = pl.ds(j * rows, rows)
+        at = lines_of(j)
         step_copy(3, j).wait_recv()
         final[:, half, at, :] = lax.select(owner_yh == yh, merged[:, at, :], cross_in[:, at, :])
         send_step(4, j)
@@ -247,7 +254,8 @@
         return [two_rows(final[u, :, at, :]).astype(F32) for u in range(2)]
 
     def reference_power(j):
-        step_copy(4, j).wait_recv()
+        while landed and starts[landed[0]] < (j + 1) * rows:
+            step_copy(4, landed.pop(0)).wait_recv()
         b_re, b_im = reference_tile(j)
         power_b[j], = patch_sums([b_re * b_re + b_im * b_im])
 
@@ -268,31 +276,8 @@
         for u in range(3):
             turned[i, u] = two_rows(looks[i, u]).T[0:32, :]
 
-    loads[1].wait()
-    stage(0)
-    pl.semaphore_wait(barrier, 6)
-    for j in range(chunks):
-        send_halo(0, j)
-    stage(1)
-    for j in range(chunks):
-        send_halo(1, j)
-    for copy in loads[2:]:
-        copy.wait()
-    build_band(0)
-    build_band(1)
-    for j in range(chunks):
-        offer_other(j)
-    for i in (2, 3):
-        stage(i)
-        for j in range(chunks):
-            send_halo(i, j)
-    for j in range(chunks):
-        offer_mine(j)
-    build_band(2)
-    build_band(3)
-
     def whole(i):
-        for j in range(chunks):
+        for j in range(pieces[i]):
             arrive(i, j)
         resample(i, None)
 
@@ -300,24 +285,37 @@
         for i in dates_now:
             look(i, j)
 
+    for copy in loads[1:]:
+        copy.wait()
+    for i in range(4):
+        stage(i)
+    pl.semaphore_wait(barrier, 6)
+    for i in range(4):
+        for j in range(pieces[i]):
+            send_halo(i, j)
+    for i in range(4):
+        build_band(i)
+    for j in range(chunks):
+        offer_other(j)
+    for j in range(chunks):
+        offer_mine(j)
     merge(0)
     merge(1)
     cross(0)
     merge(2)
-    whole(2)
     cross(1)
     merge(3)
+    whole(2)
+    cross(2)
     reference_power(0)
     looks_at(0, (0, 1, 2))
-    cross(2)
-    reference_power(1)
-    looks_at(1, (0, 1, 2))
     cross(3)
     whole(3)
+    reference_power(1)
+    looks_at(1, (0, 1, 2, 3))
+    look(3, 0)
     reference_power(2)
     looks_at(2, (0, 1, 2, 3))
-    looks_at(0, (3,))
-    looks_at(1, (3,))
     reference_power(3)
     looks_at(3, (0, 1, 2, 3))
     for i in range(4):
@@ -338,13 +336,14 @@
 def on_device(slc, shift_table, phase_table, reference_ids):
     dates_dev, lines = slc.shape[1], slc.shape[2]
     half_lines = lines // 2
-    chunks = min(CHUNKS, half_lines // 32)
-    rows = half_lines // chunks
+    chunks = len(CHUNKS)
+    blocks = half_lines // 32
+    rows = half_lines // blocks
     dates, rngs = lax.axis_size("date"), lax.axis_size("rng")
     out_half = half_lines // LOOK_AZ
     vmem = pl.BlockSpec(memory_space=pltpu.VMEM)
     found = pl.pallas_call(
-        functools.partial(kernel, dates, rngs, chunks, half_lines),
+        functools.partial(kernel, dates, rngs, CHUNKS, blocks, half_lines),
         out_shape=jax.ShapeDtypeStruct((3, 4, 32, 2 * out_half), F32),
         in_specs=[pl.BlockSpec(memory_space=pl.ANY)] * 5,
         out_specs=vmem,
@@ -365,7 +364,7 @@
             pltpu.VMEM((2, half_lines, 512), BF16),
             pltpu.VMEM((2, 2, half_lines, 512), BF16),
             pltpu.VMEM((6 * rows, 128), F32),
-            pltpu.VMEM((chunks, 2 * rows // LOOK_AZ, 128), F32),
+            pltpu.VMEM((blocks, 2 * rows // LOOK_AZ, 128), F32),
             pltpu.VMEM((4, 3, 2, out_half, 128), F32),
             pltpu.VMEM((4, 3, 32, 2 * out_half), F32),
             pltpu.SemaphoreType.DMA((5,)),

time: 40.7 us -> 39.5 us (0.971)
  Pallas kernels: 39.9 us -> 38.6 us
    pallas_call x1, Pallas kernels: 38.3 us -> 37 us  [on_device(): pl.pallas_call(functools.partial(kernel, dates, rngs, CHUNKS, blocks, hal...]
where the time goes in v3:
time: 39.5 us; the launch traced here: 39.2 us
  Pallas kernels  38.6 us (98%)
  between operations  0.64 us (2%)
    pallas_call x1, Pallas kernels, on_device(): pl.pallas_call(functools.partial(kernel, dates, rngs, CHUNKS, blocks, hal...  37 us
    pallas_call x1, Pallas kernels, on_device(): pl.pallas_call(hand_out, out_shape=(jax.ShapeDtypeStruct((2, 4, 32, 2 * o...  1.63 us

profile of v3, /device:TPU:8, one launch (start us, length us, event | category | flops | bytes accessed | tf_op | source)
XLA Modules:
  0.0 39.2 jit_solution(12619330597802866074)
XLA Ops:
  0.6 37.0 %shard_map.68.found_ref = f32[3,4,32,64]{3,2,1,0:T(8,128)} custom-call(s32[2]{0:T(128)} %ids_hbm.1, s32[4,512]{1,0:T(4,128)} %shift_hbm.1, s32[4,512]{1,0:T(4,128)} %phase_hbm.1, bf16[16,256]{1,0:T(8,128)(2,1)} %constant.10.table_hbm, bf16[2,4,2,128,512]{4,3,2,1,0:T(8,128)(2,1)} %bitcast.3), custom_call_target="tpu_custom_call" | custom-call | tf_op jit(solution)/shard_map/pallas_call | solution.py:345
  37.6 1.6 %shard_map.69 = (f32[2,4,32,64]{3,2,1,0:T(8,128)}, f32[4,32,64]{2,1,0:T(8,128)}) custom-call(f32[3,4,32,64]{3,2,1,0:T(8,128)} %shard_map.68.found_ref), custom_call_target="tpu_custom_call" | custom-call | tf_op jit(solution)/shard_map/pallas_call | solution.py:386

commit v4 on v3

--- a/solution.py
+++ b/solution.py
@@ -285,16 +285,24 @@
         for i in dates_now:
             look(i, j)
 
-    for copy in loads[1:]:
+    loads[1].wait()
+    stage(0)
+    pl.semaphore_wait(barrier, 6)
+    for j in range(chunks):
+        send_halo(0, j)
+    stage(1)
+    for j in range(chunks):
+        send_halo(1, j)
+    for copy in loads[2:]:
         copy.wait()
-    for i in range(4):
+    build_band(0)
+    build_band(1)
+    for i in (2, 3):
         stage(i)
-    pl.semaphore_wait(barrier, 6)
-    for i in range(4):
         for j in range(pieces[i]):
             send_halo(i, j)
-    for i in range(4):
-        build_band(i)
+    build_band(2)
+    build_band(3)
     for j in range(chunks):
         offer_other(j)
     for j in range(chunks):

time: 39.5 us -> 39.5 us (level)
  no operation moved by 1% of the time
where the time goes in v4:
time: 39.5 us; the launch traced here: 39.2 us
  Pallas kernels  38.6 us (98%)
  between operations  0.64 us (2%)
    pallas_call x1, Pallas kernels, on_device(): pl.pallas_call(functools.partial(kernel, dates, rngs, CHUNKS, blocks, hal...  37 us
    pallas_call x1, Pallas kernels, on_device(): pl.pallas_call(hand_out, out_shape=(jax.ShapeDtypeStruct((2, 4, 32, 2 * o...  1.63 us

profile of v4, /device:TPU:8, one launch (start us, length us, event | category | flops | bytes accessed | tf_op | source)
XLA Modules:
  0.0 39.2 jit_solution(12418337518377513383)
XLA Ops:
  0.6 37.0 %shard_map.68.found_ref = f32[3,4,32,64]{3,2,1,0:T(8,128)} custom-call(s32[2]{0:T(128)} %ids_hbm.1, s32[4,512]{1,0:T(4,128)} %shift_hbm.1, s32[4,512]{1,0:T(4,128)} %phase_hbm.1, bf16[16,256]{1,0:T(8,128)(2,1)} %constant.10.table_hbm, bf16[2,4,2,128,512]{4,3,2,1,0:T(8,128)(2,1)} %bitcast.3), custom_call_target="tpu_custom_call" | custom-call | tf_op jit(solution)/shard_map/pallas_call | solution.py:353
  37.6 1.6 %shard_map.69 = (f32[2,4,32,64]{3,2,1,0:T(8,128)}, f32[4,32,64]{2,1,0:T(8,128)}) custom-call(f32[3,4,32,64]{3,2,1,0:T(8,128)} %shard_map.68.found_ref), custom_call_target="tpu_custom_call" | custom-call | tf_op jit(solution)/shard_map/pallas_call | solution.py:394
